TPU v7x, 32 devices: a whole 2x2x4 slice. The times are simulated.
32 devices in a mesh: dp: 4 (over y, x), mp: 8 (over z, core).
Axes of the slice: x: 2, y: 2, z: 4, core: 2. Of those that a mesh axis runs over, the one named last changes fastest.
Arguments:
- activations: bfloat16 [4096, 2048], P('dp', 'mp'), may hold values from -6 to 6
- out_grad: bfloat16 [4096, 8192], P('dp'), may hold values from -0.8984375 to 0.8984375
- old_weight: bfloat16 [8, 256, 8192], P('mp', 'dp'), may hold values from -0.125 to 0.125
- old_first: float32 [8, 256, 8192], P('mp', 'dp'), may hold values from -6 to 6
- old_second: float32 [8, 256, 8192], P('mp', 'dp'), may hold values from 0.25 to 4
- step: int32 [1], replicated, may hold values from 1 to 31
- next_input: bfloat16 [4096, 2048], P('dp', 'mp'), may hold values from -6 to 6
Outputs:
- new_weight: bfloat16 [8, 344, 8192], P('mp', 'dp')
- new_first: float32 [8, 344, 8192], P('mp', 'dp')
- new_second: float32 [8, 344, 8192], P('mp', 'dp')
- output: bfloat16 [4096, 8192], P('dp', 'mp')
Inputs may be any that keep to these rules, and one draw needn't show every extreme that they name: `step`: the number of Adam steps taken, this one included.
All inputs are finite; a program needn't handle non-finite values.
Results may differ from a plain program's by a relative error of at most 0.0049.
Values may be sent and summed in bfloat16 or wider, within the bound.
A program may use at most 192 MiB of HBM per device.

v0:
```python
import jax
import jax.numpy as jnp
from jax import lax
from jax.sharding import PartitionSpec as P


def partner(i, k, n):
    return i ^ k if n & n - 1 == 0 else (i + k) % n


def exchange(block, axis, k):
    n = lax.axis_size(axis)
    return lax.ppermute(block, axis, [(i, partner(i, k, n)) for i in range(n)])


def target(k, n, axis):
    me = lax.axis_index(axis)
    return me ^ k if n & n - 1 == 0 else lax.rem(me + k, n)


def to_front(block, axis):
    n = lax.axis_size(axis)
    return lax.ppermute(block, axis, [(i, i - 1) for i in range(1, n)])


def body(activations, out_grad, old_weight, old_first, old_second, step, next_input):
    owners = lax.axis_size("dp")
    owner = lax.axis_index("dp")
    old_rows = old_weight.shape[1]
    width = old_weight.shape[2]
    held_rows = old_rows * owners
    shard_rows = (held_rows + owners - 2) // (owners - 1)
    input_all = lax.all_gather(next_input, "mp", axis=1, tiled=True)
    part = lax.dot_general(
        activations, out_grad, (((0,), (0,)), ((), ())), preferred_element_type=jnp.float32
    ).astype(jnp.bfloat16)
    part = part.reshape(owners, old_rows, width)
    grad = lax.dynamic_index_in_dim(part, owner, 0, keepdims=False).astype(jnp.float32)
    for k in range(1, owners):
        away = lax.dynamic_index_in_dim(part, target(k, owners, "dp"), 0, keepdims=False)
        grad = grad + exchange(away, "dp", k).astype(jnp.float32)
    step_float = step[0].astype(jnp.float32)
    first_fix = 1.0 - jnp.power(jnp.float32(0.9), step_float)
    second_fix = 1.0 - jnp.power(jnp.float32(0.95), step_float)
    new_first = 0.9 * old_first[0] + 0.1 * grad
    new_second = 0.95 * old_second[0] + 0.05 * grad * grad
    update = new_first / first_fix / (jnp.sqrt(new_second / second_fix) + 1e-08)
    new_weight = (old_weight[0].astype(jnp.float32) - 0.01 * update).astype(jnp.bfloat16)
    weight_part = lax.all_to_all(new_weight, "mp", split_axis=1, concat_axis=0, tiled=True)
    heads = lax.axis_size("mp")
    weight_part = weight_part.reshape(heads, old_rows, -1)
    weight_cols = lax.all_gather(weight_part, "dp", axis=1, tiled=True)
    weight_cols = weight_cols.reshape(heads * held_rows, -1)
    begin = owner * (shard_rows - old_rows)

    def mine(block):
        behind = to_front(block.astype(jnp.bfloat16), "dp").astype(block.dtype)
        rows = jnp.concatenate([block, behind, jnp.zeros((shard_rows, width), block.dtype)], 0)
        return lax.dynamic_slice_in_dim(rows, begin, shard_rows, 0)[None]

    outs = (mine(new_weight), mine(new_first), mine(new_second))
    output = jnp.dot(input_all, weight_cols, preferred_element_type=jnp.float32).astype(
        jnp.bfloat16
    )
    return (*outs, output)


def solution(mesh):
    return jax.shard_map(
        body,
        mesh=mesh,
        in_specs=(
            P("dp", "mp"),
            P("dp", None),
            P("mp", "dp", None),
            P("mp", "dp", None),
            P("mp", "dp", None),
            P(),
            P("dp", "mp"),
        ),
        out_specs=(P("mp", "dp", None), P("mp", "dp", None), P("mp", "dp", None), P("dp", "mp")),
        check_vma=False,
    )
```

profile of v0, /device:TPU:0, one launch (start us, length us, event | category | flops | bytes accessed | tf_op | source)
XLA Modules:
  0.0 292.9 jit_solution(17170010049314651664)
XLA Ops:
  7.2 0.0 copy-start
  7.2 0.0 all-gather.3.cloned.1.call-start
  7.2 1.0 copy-done
  8.2 10.7 %convolution_convert_fusion = bf16[256,8192]{1,0:T(8,128)(2,1)S(1)} fusion(bf16[1024,256]{1,0:T(8,128)(2,1)S(1)} %copy-done, bf16[1024,8192]{1,0:T(8,128)(2,1)} %param.8), kind=kOutput, calls=%fused_computation | convolution fusion | flops 4297064448 | bytes 21495808 | tf_op jit(solution)/shard_map/dot_general | solution.py:34
  19.0 0.0 copy-start.4
  19.0 1.8 dynamic-slice_bitcast_fusion.2
  20.7 1.2 copy-done.4
  21.9 2.9 %collective-permute-start = (bf16[64,8192]{1,0:T(8,128)(2,1)}, bf16[64,8192]{1,0:T(8,128)(2,1)S(1)}, u32[]{:S(2)}, u32[]{:S(2)}) collective-permute-start(bf16[64,8192]{1,0:T(8,128)(2,1)} %get-tuple-element.26), channel_id=1, source_target_pairs={{0,8},{8,0},{16,24},{24,16},{1,9},{9,1},{17,25},{25,17},{2,10},{10... | collective-permute-start | bytes 3145736 | tf_op jit(solution)/shard_map/ppermute | solution.py:13
  24.8 1.5 collective-permute-start.1
  26.4 0.0 collective-permute-start.2
  27.1 0.0 copy-start.9
  27.1 21.9 %collective-permute-done = bf16[64,8192]{1,0:T(8,128)(2,1)S(1)} collective-permute-done((bf16[64,8192]{1,0:T(8,128)(2,1)}, bf16[64,8192]{1,0:T(8,128)(2,1)S(1)}, u32[]{:S(2)}, u32[]{:S(2)}) %collective-permute-start) | collective-permute-done | bytes 1048608 | tf_op jit(solution)/shard_map/ppermute | solution.py:13
  49.0 23.1 %collective-permute-done.1 = bf16[64,8192]{1,0:T(8,128)(2,1)S(1)} collective-permute-done((bf16[64,8192]{1,0:T(8,128)(2,1)}, bf16[64,8192]{1,0:T(8,128)(2,1)S(1)}, u32[]{:S(2)}, u32[]{:S(2)}) %collective-permute-start.1) | collective-permute-done | bytes 1048608 | tf_op jit(solution)/shard_map/ppermute | solution.py:13
  72.1 0.0 copy-done.7
  72.2 1.0 copy-done.8
  73.1 0.0 collective-permute-done.2
  73.1 5.9 %fusion.11 = (bf16[64,8192]{1,0:T(8,128)(2,1)}, f32[64,8192]{1,0:T(8,128)S(1)}, bf16[64,8192]{1,0:T(8,128)(2,1)}, f32[64,8192]{1,0:T(8,128)S(1)}) fusion(bf16[64,8192]{1,0:T(8,128)(2,1)} %collective-permute-done.2, bf16[64,8192]{1,0:T(8,128)(2,1)} %copy-done.8, bf16[64,8192]{1,0:T(8,128)(2,1)} %copy-done.7, bf16[4,64,8192]{2,1,0:T(8,128)(2,1)} %bitcast.42, ...), kind=kLoop, calls=%fused_computation.29 | loop fusion | flops 8388608 | bytes 14680068 | tf_op jit(solution)/shard_map/convert_element_type | solution.py:57
  79.0 0.0 copy-done.9
  79.0 1.1 fusion.7
  80.1 0.2 copy-done.2
  80.3 0.1 copy.21
  80.4 31.3 %all_to_all.16 = bf16[64,8,1024]{2,0,1:T(8,128)(2,1)S(1)} all-to-all(bf16[64,8,1024]{2,0,1:T(8,128)(2,1)S(1)} %bitcast.46), channel_id=1, replica_groups=mesh['dp'=4,'mp'=8] {'mp'}, dimensions={1} | all-to-all | bytes 2097152 | tf_op jit(solution)/shard_map/all_to_all | solution.py:49
  111.7 1.5 copy.16
  113.2 0.0 all-gather.3.cloned.1.call-update
  113.2 0.0 all-gather.5.cloned.1.call-start
  113.3 0.7 all-gather.5.cloned.1.call-update
  114.0 1.3 collective-permute-start.4
  115.3 1.3 collective-permute-start.5
  116.6 0.1 pad_dynamic-slice_fusion.6
  116.7 0.1 pad_dynamic-slice_fusion.7
  116.8 1.5 collective-permute-start.3
  118.2 35.3 %collective-permute-done.4 = bf16[64,8192]{1,0:T(8,128)(2,1)} collective-permute-done((bf16[64,8192]{1,0:T(8,128)(2,1)}, bf16[64,8192]{1,0:T(8,128)(2,1)}, u32[]{:S(2)}, u32[]{:S(2)}) %collective-permute-start.4) | collective-permute-done | bytes 1048608 | tf_op jit(solution)/shard_map/ppermute | solution.py:23
  153.5 1.4 convert_element_type.60
  154.9 0.0 copy-start.3
  154.9 21.1 %collective-permute-done.5 = bf16[64,8192]{1,0:T(8,128)(2,1)} collective-permute-done((bf16[64,8192]{1,0:T(8,128)(2,1)}, bf16[64,8192]{1,0:T(8,128)(2,1)}, u32[]{:S(2)}, u32[]{:S(2)}) %collective-permute-start.5) | collective-permute-done | bytes 1048608 | tf_op jit(solution)/shard_map/ppermute | solution.py:23
  176.0 1.4 convert_element_type.62
  177.4 0.0 copy-done.3
  177.4 4.0 %fusion.1 = (f32[86,8192]{1,0:T(8,128)}, f32[86,8192]{1,0:T(8,128)}) fusion(s32[]{:T(128)S(6)} %select_n.22, f32[64,8192]{1,0:T(8,128)S(1)} %get-tuple-element.21, f32[64,8192]{1,0:T(8,128)S(1)} %convert_element_type.62, f32[86]{0:T(128)S(1)} %pad_dynamic-slice_fusion.6, f32[64,8192]{1,0:T(8,128)S(1)} %convert_element_type.60, f32[64,8192]{1,0:T(8,128)S(1)} %copy-done.3), kind=kLoop, calls=%fused_computation.9 | loop fusion | flops 2818048 | bytes 14025052 | tf_op jit(solution)/shard_map/concatenate | solution.py:58
  181.3 6.7 %broadcast_in_dim.14 = f32[1,86,8192]{2,0,1:T(1,128)} reshape(f32[86,8192]{1,0:T(8,128)} %get-tuple-element.30) | data formatting | bytes 5636096 | tf_op jit(solution)/shard_map/broadcast_in_dim | solution.py:59
  188.0 0.0 copy-done.5
  188.0 4.7 %broadcast_in_dim.15 = f32[1,86,8192]{2,0,1:T(1,128)} reshape(f32[86,8192]{1,0:T(8,128)S(1)} %copy-done.5) | data formatting | bytes 5636096 | tf_op jit(solution)/shard_map/broadcast_in_dim | solution.py:59
  192.8 4.1 %collective-permute-done.3 = bf16[64,8192]{1,0:T(8,128)(2,1)} collective-permute-done((bf16[64,8192]{1,0:T(8,128)(2,1)}, bf16[64,8192]{1,0:T(8,128)(2,1)}, u32[]{:S(2)}, u32[]{:S(2)}) %collective-permute-start.3) | collective-permute-done | bytes 1048608 | tf_op jit(solution)/shard_map/ppermute | solution.py:23
  196.9 3.4 %fusion.10 = bf16[1,86,8192]{2,1,0:T(8,128)(2,1)} fusion(s32[]{:T(128)S(6)} %select_n.22, bf16[64,8192]{1,0:T(8,128)(2,1)} %copy-done.6, bf16[64,8192]{1,0:T(8,128)(2,1)} %collective-permute-done.3, bf16[86]{0:T(256)(128)(2,1)S(1)} %pad_dynamic-slice_fusion.7), kind=kLoop, calls=%fused_computation.22 | loop fusion | flops 4227072 | bytes 3506352 | tf_op jit(solution)/shard_map/broadcast_in_dim | solution.py:59
  200.3 25.5 %all-gather.3.cloned.1.call-done = bf16[8,256,1024]{2,0,1:T(8,128)(2,1)} async-done(((bf16[8,64,1024]{2,0,1:T(8,128)(2,1)}), bf16[8,256,1024]{2,0,1:T(8,128)(2,1)}) %all-gather.3.cloned.1.call-update) | async-done | bytes 4194320 | tf_op jit(solution)/shard_map/all_gather | solution.py:52
  225.8 6.5 %copy.17 = bf16[8,256,1024]{2,1,0:T(8,128)(2,1)} copy(bf16[8,256,1024]{2,0,1:T(8,128)(2,1)} %all-gather.3.cloned.1.call-done) | data formatting | bytes 8388608 | tf_op jit(solution)/shard_map/all_gather | solution.py:52
  232.3 42.9 %all-gather.5.cloned.1.call-done = bf16[1024,2048]{1,0:T(8,128)(2,1)} async-done(((bf16[1024,256]{1,0:T(8,128)(2,1)}), bf16[1024,2048]{1,0:T(8,128)(2,1)}) %all-gather.5.cloned.1.call-update) | async-done | bytes 4194320 | tf_op jit(solution)/shard_map/all_gather | solution.py:33
  275.2 8.3 %convert_bitcast_fusion = bf16[1024,1024]{0,1:T(8,128)(2,1)S(1)} fusion(bf16[2048,1024]{1,0:T(8,128)(2,1)} %bitcast.44, bf16[1024,2048]{1,0:T(8,128)(2,1)} %all-gather.5.cloned.1.call-done), kind=kOutput, calls=%fused_computation.19 | convolution fusion | flops 4296015872 | bytes 10485760 | tf_op jit(solution)/shard_map/dot_general | solution.py:62
  283.5 2.6 copy.18
  (10 shorter events, 0.0 us)
Async XLA Ops:
  7.2 1.1 copy-start
  7.2 218.6 %all-gather.3.cloned.1.call-start = ((), (), s32[]{:S(2)}) async-start(), calls=%async_computation.1 | async-start | bytes 5242880 | tf_op jit(solution)/shard_map/all_gather | solution.py:52
  19.0 2.9 %copy-start.4 = (bf16[256,8192]{1,0:T(8,128)(2,1)}, bf16[256,8192]{1,0:T(8,128)(2,1)S(1)}, u32[]{:S(2)}) copy-start(bf16[256,8192]{1,0:T(8,128)(2,1)S(1)} %convolution_convert_fusion) | copy-start | bytes 12582916
  21.9 27.1 %collective-permute-start = (bf16[64,8192]{1,0:T(8,128)(2,1)}, bf16[64,8192]{1,0:T(8,128)(2,1)S(1)}, u32[]{:S(2)}, u32[]{:S(2)}) collective-permute-start(bf16[64,8192]{1,0:T(8,128)(2,1)} %get-tuple-element.26), channel_id=1, source_target_pairs={{0,8},{8,0},{16,24},{24,16},{1,9},{9,1},{17,25},{25,17},{2,10},{10... | collective-permute-start | bytes 3145736 | tf_op jit(solution)/shard_map/ppermute | solution.py:13
  24.8 47.3 %collective-permute-start.1 = (bf16[64,8192]{1,0:T(8,128)(2,1)}, bf16[64,8192]{1,0:T(8,128)(2,1)S(1)}, u32[]{:S(2)}, u32[]{:S(2)}) collective-permute-start(bf16[64,8192]{1,0:T(8,128)(2,1)} %get-tuple-element.28), channel_id=1, source_target_pairs={{0,16},{8,24},{16,0},{24,8},{1,17},{9,25},{17,1},{25,9},{2,18},{10... | collective-permute-start | bytes 3145736 | tf_op jit(solution)/shard_map/ppermute | solution.py:13
  26.4 46.8 %collective-permute-start.2 = (bf16[64,8192]{1,0:T(8,128)(2,1)}, bf16[64,8192]{1,0:T(8,128)(2,1)}, u32[]{:S(2)}, u32[]{:S(2)}) collective-permute-start(bf16[64,8192]{1,0:T(8,128)(2,1)} %get-tuple-element.27), channel_id=1, source_target_pairs={{0,24},{8,16},{16,8},{24,0},{1,25},{9,17},{17,9},{25,1},{2,26},{10... | collective-permute-start | bytes 3145736 | tf_op jit(solution)/shard_map/ppermute | solution.py:13
  27.1 51.9 %copy-start.9 = (bf16[1,64,8192]{2,1,0:T(8,128)(2,1)S(1)}, bf16[1,64,8192]{2,1,0:T(8,128)(2,1)}, u32[]{:S(2)}) copy-start(bf16[1,64,8192]{2,1,0:T(8,128)(2,1)} %param.9) | copy-start | bytes 3145732
  49.0 23.1 %copy-start.7 = (bf16[64,8192]{1,0:T(8,128)(2,1)}, bf16[64,8192]{1,0:T(8,128)(2,1)S(1)}, u32[]{:S(2)}) copy-start(bf16[64,8192]{1,0:T(8,128)(2,1)S(1)} %collective-permute-done) | copy-start | bytes 3145732
  72.2 1.0 copy-start.8
  79.0 1.3 copy-start.2
  80.3 31.4 %copy-start.6 = (bf16[64,8192]{1,0:T(8,128)(2,1)}, bf16[64,8192]{1,0:T(8,128)(2,1)S(1)}, u32[]{:S(2)}) copy-start(bf16[64,8192]{1,0:T(8,128)(2,1)S(1)} %fusion.7) | copy-start | bytes 3145732
  113.2 162.0 %all-gather.5.cloned.1.call-start = ((), (), s32[]{:S(2)}) async-start(), calls=%async_computation.2 | async-start | bytes 4718592 | tf_op jit(solution)/shard_map/all_gather | solution.py:33
  114.0 39.5 %collective-permute-start.4 = (bf16[64,8192]{1,0:T(8,128)(2,1)}, bf16[64,8192]{1,0:T(8,128)(2,1)}, u32[]{:S(2)}, u32[]{:S(2)}) collective-permute-start(bf16[64,8192]{1,0:T(8,128)(2,1)} %get-tuple-element.24), channel_id=1, source_target_pairs={{8,0},{16,8},{24,16},{9,1},{17,9},{25,17},{10,2},{18,10},{26,18},{... | collective-permute-start | bytes 3145736 | tf_op jit(solution)/shard_map/ppermute | solution.py:23
  115.3 60.7 %collective-permute-start.5 = (bf16[64,8192]{1,0:T(8,128)(2,1)}, bf16[64,8192]{1,0:T(8,128)(2,1)}, u32[]{:S(2)}, u32[]{:S(2)}) collective-permute-start(bf16[64,8192]{1,0:T(8,128)(2,1)} %get-tuple-element.20), channel_id=1, source_target_pairs={{8,0},{16,8},{24,16},{9,1},{17,9},{25,17},{10,2},{18,10},{26,18},{... | collective-permute-start | bytes 3145736 | tf_op jit(solution)/shard_map/ppermute | solution.py:23
  116.8 80.1 %collective-permute-start.3 = (bf16[64,8192]{1,0:T(8,128)(2,1)}, bf16[64,8192]{1,0:T(8,128)(2,1)}, u32[]{:S(2)}, u32[]{:S(2)}) collective-permute-start(bf16[64,8192]{1,0:T(8,128)(2,1)} %copy-done.6), channel_id=1, source_target_pairs={{8,0},{16,8},{24,16},{9,1},{17,9},{25,17},{10,2},{18,10},{26,18},{... | collective-permute-start | bytes 3145736 | tf_op jit(solution)/shard_map/ppermute | solution.py:23
  154.9 22.5 %copy-start.3 = (f32[64,8192]{1,0:T(8,128)S(1)}, f32[64,8192]{1,0:T(8,128)}, u32[]{:S(2)}) copy-start(f32[64,8192]{1,0:T(8,128)} %copy-done.2) | copy-start | bytes 6291460
  181.3 6.7 %copy-start.5 = (f32[86,8192]{1,0:T(8,128)S(1)}, f32[86,8192]{1,0:T(8,128)}, u32[]{:S(2)}) copy-start(f32[86,8192]{1,0:T(8,128)} %get-tuple-element.29) | copy-start | bytes 8454148
  275.2 10.9 %copy-start.1 = (bf16[1024,256]{1,0:T(8,128)(2,1)S(1)}, bf16[1024,256]{1,0:T(8,128)(2,1)}, u32[]{:S(2)}) copy-start(bf16[1024,256]{1,0:T(8,128)(2,1)} %param.7) | copy-start | bytes 1572868
Sparse Core Ops, SparseCore 0:
  113.3 112.3 all-gather.2
  227.4 47.7 all-gather.4
where the time goes:
time: 293 us
  waiting for transfers between devices  175 us (60%)
  blocking collectives  31.3 us (11%)
  local copies, waits for them, and re-layouts  27.4 us (9%)
  matrix products  19 us (6%)
  other arithmetic  17 us (6%)
  between operations  14.9 us (5%)
  starting transfers between devices  8.58 us (3%)
    ppermute x3, waiting for transfers between devices, to_front(): return lax.ppermute(block, axis, [(i, i - 1) for i in range(1, n)])  60.5 us
    ppermute x3, waiting for transfers between devices, exchange(): return lax.ppermute(block, axis, [(i, partner(i, k, n)) for i in range(n)])  45 us
    all_gather x1, waiting for transfers between devices, body(): input_all = lax.all_gather(next_input, 'mp', axis=1, tiled=True)  42.9 us
    all_to_all x1, blocking collectives, body(): lax.all_to_all(new_weight, 'mp', split_axis=1, concat_axis=0, tiled=True)  31.3 us
    all_gather x1, waiting for transfers between devices, body(): weight_cols = lax.all_gather(weight_part, 'dp', axis=1, tiled=True)  25.5 us
    broadcast_in_dim x2, local copies, waits for them, and re-layouts, mine(): return lax.dynamic_slice_in_dim(rows, begin, shard_rows, 0)[None]  11.4 us
    dot_general x1, matrix products, body(): lax.dot_general(activations, out_grad, (((0,), (0,)), ((), ())), preferre...  10.7 us
    convert_element_type x3, other arithmetic, mine(): behind = to_front(block.astype(jnp.bfloat16), 'dp').astype(block.dtype)  8.57 us
  transfers between devices with their start and end apart: 8, of which 7 were waited for; matrix products, arithmetic and copies ran while one was open for 10% of the time, Pallas kernels for 0%

commit v1 on v0

--- a/solution.py
+++ b/solution.py
@@ -49,7 +49,21 @@
     weight_part = lax.all_to_all(new_weight, "mp", split_axis=1, concat_axis=0, tiled=True)
     heads = lax.axis_size("mp")
     weight_part = weight_part.reshape(heads, old_rows, -1)
-    weight_cols = lax.all_gather(weight_part, "dp", axis=1, tiled=True)
+    ways, here, step_2 = (lax.axis_size("dp"), lax.axis_index("dp"), weight_part.shape[1])
+    dims = [n_2 * ways if d == 1 else n_2 for d, n_2 in enumerate(weight_part.shape)]
+    full = lax.dynamic_update_slice_in_dim(
+        jnp.zeros(dims, weight_part.dtype), weight_part, here * step_2, axis=1
+    )
+    going_up = going_down = weight_part
+    for far in range(1, ways // 2 + 1):
+        going_up = lax.ppermute(going_up, "dp", [(d, (d + 1) % ways) for d in range(ways)])
+        full = lax.dynamic_update_slice_in_dim(full, going_up, (here - far) % ways * step_2, axis=1)
+        if 2 * far < ways:
+            going_down = lax.ppermute(going_down, "dp", [(d, (d - 1) % ways) for d in range(ways)])
+            full = lax.dynamic_update_slice_in_dim(
+                full, going_down, (here + far) % ways * step_2, axis=1
+            )
+    weight_cols = full
     weight_cols = weight_cols.reshape(heads * held_rows, -1)
     begin = owner * (shard_rows - old_rows)
 

time: 293 us -> 250 us (0.85)
  waiting for transfers between devices: 175 us -> 143 us
  blocking collectives: 31.3 us -> 0 us
  starting transfers between devices: 8.58 us -> 16.3 us
  local copies, waits for them, and re-layouts: 27.4 us -> 33.7 us
  other arithmetic: 17 us -> 21.6 us
    ppermute x0 -> x3, waiting for transfers between devices: none -> 54.8 us  [the longest x2 54.8 us: body(): lax.ppermute(going_up, 'dp', [(d, (d + 1) % ways) for d in range(ways)])]
    all_gather x1, waiting for transfers between devices: 42.9 us -> 0.01 us  [body(): input_all = lax.all_gather(next_input, 'mp', axis=1, tiled=True)]
    all_to_all x1 -> x0, blocking collectives: 31.3 us -> none  [body(): lax.all_to_all(new_weight, 'mp', split_axis=1, concat_axis=0, tiled=True)]
    all_gather x1 -> x0, waiting for transfers between devices: 25.5 us -> none  [body(): weight_cols = lax.all_gather(weight_part, 'dp', axis=1, tiled=True)]
    ppermute x3, waiting for transfers between devices: 60.5 us -> 43.8 us  [to_front(): return lax.ppermute(block, axis, [(i, i - 1) for i in range(1, n)])]
    dynamic_update_slice x0 -> x4, local copies, waits for them, and re-layouts: none -> 9.16 us  [the longest x2 4.63 us: body(): lax.dynamic_update_slice_in_dim(full, going_up, (here - far) % ways * ste...]
    all_gather x1 -> x0, local copies, waits for them, and re-layouts: 6.49 us -> none  [body(): weight_cols = lax.all_gather(weight_part, 'dp', axis=1, tiled=True)]
    all_to_all x0 -> x1, starting transfers between devices: none -> 4.98 us  [body(): lax.all_to_all(new_weight, 'mp', split_axis=1, concat_axis=0, tiled=True)]
  transfers between devices with their start and end apart: 8 -> 11, of which waited for: 7 -> 6; matrix products, arithmetic and copies ran while one was open for 10% -> 18% of each run, Pallas kernels for 0% -> 0%
where the time goes in v1:
time: 250 us
  waiting for transfers between devices  143 us (57%)
  local copies, waits for them, and re-layouts  33.7 us (13%)
  other arithmetic  21.6 us (9%)
  matrix products  20.2 us (8%)
  starting transfers between devices  16.3 us (7%)
  between operations  14.9 us (6%)
    ppermute x2, waiting for transfers between devices, body(): lax.ppermute(going_up, 'dp', [(d, (d + 1) % ways) for d in range(ways)])  54.8 us
    ppermute x3, waiting for transfers between devices, exchange(): return lax.ppermute(block, axis, [(i, partner(i, k, n)) for i in range(n)])  44.5 us
    ppermute x3, waiting for transfers between devices, to_front(): return lax.ppermute(block, axis, [(i, i - 1) for i in range(1, n)])  43.8 us
    dot_general x1, matrix products, body(): lax.dot_general(activations, out_grad, (((0,), (0,)), ((), ())), preferre...  12.1 us
    broadcast_in_dim x2, local copies, waits for them, and re-layouts, mine(): return lax.dynamic_slice_in_dim(rows, begin, shard_rows, 0)[None]  11.4 us
    convert_element_type x3, other arithmetic, mine(): behind = to_front(block.astype(jnp.bfloat16), 'dp').astype(block.dtype)  11.3 us
    dot_general x1, matrix products, body(): jnp.dot(input_all, weight_cols, preferred_element_type=jnp.float32)  8.05 us
    concatenate x1, other arithmetic, mine(): jnp.concatenate([block, behind, jnp.zeros((shard_rows, width), block.dtyp...  6.12 us
  transfers between devices with their start and end apart: 11, of which 6 were waited for; matrix products, arithmetic and copies ran while one was open for 18% of the time, Pallas kernels for 0%

profile of v1, /device:TPU:0, one launch (start us, length us, event | category | flops | bytes accessed | tf_op | source)
XLA Modules:
  0.0 249.7 jit_solution(3338454532970665787)
XLA Ops:
  7.2 0.0 copy-start
  7.2 0.0 all-gather.2.cloned.1.call-start
  7.2 1.0 copy-done
  8.2 12.1 %convolution_convert_fusion = bf16[256,8192]{1,0:T(8,128)(2,1)} fusion(bf16[1024,256]{1,0:T(8,128)(2,1)S(1)} %copy-done, bf16[1024,8192]{1,0:T(8,128)(2,1)} %param.8), kind=kOutput, calls=%fused_computation | convolution fusion | flops 4297064448 | bytes 21495808 | tf_op jit(solution)/shard_map/dot_general | solution.py:34
  20.3 3.6 %dynamic-slice_bitcast_fusion.2 = (bf16[64,8192]{1,0:T(8,128)(2,1)}, bf16[64,8192]{1,0:T(8,128)(2,1)}, bf16[64,8192]{1,0:T(8,128)(2,1)}) fusion(bf16[4,64,8192]{2,1,0:T(8,128)(2,1)} %bitcast.42, s32[]{:T(128)S(6)} %select_n.46, s32[]{:T(128)S(6)} %select_n.48, s32[]{:T(128)S(6)} %select_n.47), kind=kLoop, calls=%fused_computation.26 | loop fusion | bytes 6291468 | tf_op jit(solution)/shard_map/jit(dynamic_index_in_dim)/squeeze | solution.py:40
  23.9 3.9 %collective-permute-start.2 = (bf16[64,8192]{1,0:T(8,128)(2,1)}, bf16[64,8192]{1,0:T(8,128)(2,1)S(1)}, u32[]{:S(2)}, u32[]{:S(2)}) collective-permute-start(bf16[64,8192]{1,0:T(8,128)(2,1)} %get-tuple-element.27), channel_id=1, source_target_pairs={{0,24},{8,16},{16,8},{24,0},{1,25},{9,17},{17,9},{25,1},{2,26},{10... | collective-permute-start | bytes 3145736 | tf_op jit(solution)/shard_map/ppermute | solution.py:13
  27.8 0.5 collective-permute-start.1
  28.3 0.1 collective-permute-start
  28.4 0.0 all-gather.2.cloned.1.call-update
  29.1 0.0 copy-start.8
  29.2 22.9 %collective-permute-done.2 = bf16[64,8192]{1,0:T(8,128)(2,1)S(1)} collective-permute-done((bf16[64,8192]{1,0:T(8,128)(2,1)}, bf16[64,8192]{1,0:T(8,128)(2,1)S(1)}, u32[]{:S(2)}, u32[]{:S(2)}) %collective-permute-start.2) | collective-permute-done | bytes 1048608 | tf_op jit(solution)/shard_map/ppermute | solution.py:13
  52.1 21.6 %collective-permute-done.1 = bf16[64,8192]{1,0:T(8,128)(2,1)S(1)} collective-permute-done((bf16[64,8192]{1,0:T(8,128)(2,1)}, bf16[64,8192]{1,0:T(8,128)(2,1)S(1)}, u32[]{:S(2)}, u32[]{:S(2)}) %collective-permute-start.1) | collective-permute-done | bytes 1048608 | tf_op jit(solution)/shard_map/ppermute | solution.py:13
  73.7 1.0 copy-done.7
  74.6 0.0 collective-permute-done
  74.6 5.9 %fusion.11 = (bf16[64,8192]{1,0:T(8,128)(2,1)}, f32[64,8192]{1,0:T(8,128)S(1)}, bf16[64,8192]{1,0:T(8,128)(2,1)}, f32[64,8192]{1,0:T(8,128)S(1)}) fusion(bf16[64,8192]{1,0:T(8,128)(2,1)} %copy-done.6, bf16[64,8192]{1,0:T(8,128)(2,1)} %copy-done.7, bf16[64,8192]{1,0:T(8,128)(2,1)} %collective-permute-done, bf16[4,64,8192]{2,1,0:T(8,128)(2,1)} %bitcast.43, ...), kind=kLoop, calls=%fused_computation.33 | loop fusion | flops 8388608 | bytes 14680068 | tf_op jit(solution)/shard_map/convert_element_type | solution.py:71
  80.6 1.1 fusion.7
  81.7 0.2 copy-done.2
  81.9 1.0 copy-done.4
  82.9 1.1 copy.22
  83.9 5.0 %all-to-all-start = ((bf16[64,8,1024]{2,0,1:T(8,128)(2,1)}), bf16[64,8,1024]{2,0,1:T(8,128)(2,1)}, u32[]{:S(2)}, u32[]{:S(2)}) async-start(bf16[64,8,1024]{2,0,1:T(8,128)(2,1)} %bitcast.45), calls=%async_computation | async-start | bytes 2097152 | tf_op jit(solution)/shard_map/all_to_all | solution.py:49
  88.9 1.3 collective-permute-start.5
  90.2 1.3 collective-permute-start.4
  91.6 0.1 pad_dynamic-slice_fusion.7
  91.7 0.1 pad_dynamic-slice_fusion.6
  91.7 1.3 collective-permute-start.3
  93.0 24.0 %collective-permute-done.5 = bf16[64,8192]{1,0:T(8,128)(2,1)} collective-permute-done((bf16[64,8192]{1,0:T(8,128)(2,1)}, bf16[64,8192]{1,0:T(8,128)(2,1)}, u32[]{:S(2)}, u32[]{:S(2)}) %collective-permute-start.5) | collective-permute-done | bytes 1048608 | tf_op jit(solution)/shard_map/ppermute | solution.py:23
  117.1 2.7 %convert_element_type.62 = f32[64,8192]{1,0:T(8,128)} convert(bf16[64,8192]{1,0:T(8,128)(2,1)} %collective-permute-done.5) | non-fusion elementwise | flops 524288 | bytes 3145728 | tf_op jit(solution)/shard_map/convert_element_type | solution.py:71
  119.7 19.8 %collective-permute-done.4 = bf16[64,8192]{1,0:T(8,128)(2,1)} collective-permute-done((bf16[64,8192]{1,0:T(8,128)(2,1)}, bf16[64,8192]{1,0:T(8,128)(2,1)}, u32[]{:S(2)}, u32[]{:S(2)}) %collective-permute-start.4) | collective-permute-done | bytes 1048608 | tf_op jit(solution)/shard_map/ppermute | solution.py:23
  139.5 2.7 %convert_element_type.60 = f32[64,8192]{1,0:T(8,128)} convert(bf16[64,8192]{1,0:T(8,128)(2,1)} %collective-permute-done.4) | non-fusion elementwise | flops 524288 | bytes 3145728 | tf_op jit(solution)/shard_map/convert_element_type | solution.py:71
  142.2 0.0 all-to-all-done
  142.2 2.4 collective-permute-start.6
  144.6 6.1 %fusion.1 = (f32[86,8192]{1,0:T(8,128)}, f32[86,8192]{1,0:T(8,128)}) fusion(s32[]{:T(128)S(6)} %select_n.49, f32[64,8192]{1,0:T(8,128)S(1)} %get-tuple-element.21, f32[64,8192]{1,0:T(8,128)} %convert_element_type.62, f32[86]{0:T(128)S(1)} %pad_dynamic-slice_fusion.6, f32[64,8192]{1,0:T(8,128)} %convert_element_type.60, f32[64,8192]{1,0:T(8,128)} %copy-done.2), kind=kLoop, calls=%fused_computation.9 | loop fusion | flops 2818048 | bytes 14025052 | tf_op jit(solution)/shard_map/concatenate | solution.py:72
  150.7 0.5 collective-permute-start.7
  151.3 34.2 %collective-permute-done.6 = bf16[8,64,1024]{2,1,0:T(8,128)(2,1)} collective-permute-done((bf16[8,64,1024]{2,1,0:T(8,128)(2,1)}, bf16[8,64,1024]{2,1,0:T(8,128)(2,1)}, u32[]{:S(2)}, u32[]{:S(2)}) %collective-permute-start.6) | collective-permute-done | bytes 1048608 | tf_op jit(solution)/shard_map/ppermute | solution.py:59
  185.4 0.0 collective-permute-start.8
  185.4 0.0 collective-permute-done.3
  185.4 3.1 %fusion.10 = bf16[1,86,8192]{2,1,0:T(8,128)(2,1)} fusion(s32[]{:T(128)S(6)} %select_n.49, bf16[64,8192]{1,0:T(8,128)(2,1)S(1)} %copy-done.5, bf16[64,8192]{1,0:T(8,128)(2,1)} %collective-permute-done.3, bf16[86]{0:T(256)(128)(2,1)S(1)} %pad_dynamic-slice_fusion.7), kind=kLoop, calls=%fused_computation.22 | loop fusion | flops 4227072 | bytes 3506352 | tf_op jit(solution)/shard_map/broadcast_in_dim | solution.py:73
  188.5 6.7 %broadcast_in_dim.17 = f32[1,86,8192]{2,0,1:T(1,128)} reshape(f32[86,8192]{1,0:T(8,128)} %get-tuple-element.30) | data formatting | bytes 5636096 | tf_op jit(solution)/shard_map/broadcast_in_dim | solution.py:73
  195.2 4.7 %broadcast_in_dim.18 = f32[1,86,8192]{2,0,1:T(1,128)} reshape(f32[86,8192]{1,0:T(8,128)S(1)} %copy-done.3) | data formatting | bytes 5636096 | tf_op jit(solution)/shard_map/broadcast_in_dim | solution.py:73
  200.0 2.5 %broadcast_in_dim.19 = bf16[8,256,1024]{2,1,0:T(8,128)(2,1)} broadcast(bf16[]{:T(256)} %constant.73.clone.1), dimensions={} | broadcast | bytes 4194306 | tf_op jit(solution)/shard_map/broadcast_in_dim | solution.py:55
  202.5 2.3 constant_dynamic-update-slice_fusion.3
  204.8 2.3 constant_dynamic-update-slice_fusion.2
  207.1 0.0 collective-permute-done.7
  207.1 2.3 constant_dynamic-update-slice_fusion.1
  209.4 20.6 %collective-permute-done.8 = bf16[8,64,1024]{2,1,0:T(8,128)(2,1)} collective-permute-done((bf16[8,64,1024]{2,1,0:T(8,128)(2,1)}, bf16[8,64,1024]{2,1,0:T(8,128)(2,1)}, u32[]{:S(2)}, u32[]{:S(2)}) %collective-permute-start.8) | collective-permute-done | bytes 1048608 | tf_op jit(solution)/shard_map/ppermute | solution.py:59
  230.0 2.3 constant_dynamic-update-slice_fusion
  232.3 8.0 %convert_bitcast_fusion = bf16[1024,1024]{0,1:T(8,128)(2,1)S(1)} fusion(bf16[2048,1024]{1,0:T(8,128)(2,1)} %bitcast.12, bf16[1024,2048]{1,0:T(8,128)(2,1)} %all-gather.2.cloned.1.call-done), kind=kOutput, calls=%fused_computation.19 | convolution fusion | flops 4296015872 | bytes 10485760 | tf_op jit(solution)/shard_map/dot_general | solution.py:76
  240.3 2.6 %copy.19 = bf16[1024,1024]{1,0:T(8,128)(2,1)} copy(bf16[1024,1024]{0,1:T(8,128)(2,1)S(1)} %convert_bitcast_fusion) | data formatting | bytes 4194304
  (15 shorter events, 0.0 us)
Async XLA Ops:
  7.2 1.1 copy-start
  7.2 225.1 %all-gather.2.cloned.1.call-start = ((), (), s32[]{:S(2)}) async-start(), calls=%async_computation.1 | async-start | bytes 4718592 | tf_op jit(solution)/shard_map/all_gather | solution.py:33
  23.9 28.1 %collective-permute-start.2 = (bf16[64,8192]{1,0:T(8,128)(2,1)}, bf16[64,8192]{1,0:T(8,128)(2,1)S(1)}, u32[]{:S(2)}, u32[]{:S(2)}) collective-permute-start(bf16[64,8192]{1,0:T(8,128)(2,1)} %get-tuple-element.27), channel_id=1, source_target_pairs={{0,24},{8,16},{16,8},{24,0},{1,25},{9,17},{17,9},{25,1},{2,26},{10... | collective-permute-start | bytes 3145736 | tf_op jit(solution)/shard_map/ppermute | solution.py:13
  27.8 45.8 %collective-permute-start.1 = (bf16[64,8192]{1,0:T(8,128)(2,1)}, bf16[64,8192]{1,0:T(8,128)(2,1)S(1)}, u32[]{:S(2)}, u32[]{:S(2)}) collective-permute-start(bf16[64,8192]{1,0:T(8,128)(2,1)} %get-tuple-element.28), channel_id=1, source_target_pairs={{0,16},{8,24},{16,0},{24,8},{1,17},{9,25},{17,1},{25,9},{2,18},{10... | collective-permute-start | bytes 3145736 | tf_op jit(solution)/shard_map/ppermute | solution.py:13
  28.3 46.3 %collective-permute-start = (bf16[64,8192]{1,0:T(8,128)(2,1)}, bf16[64,8192]{1,0:T(8,128)(2,1)}, u32[]{:S(2)}, u32[]{:S(2)}) collective-permute-start(bf16[64,8192]{1,0:T(8,128)(2,1)} %get-tuple-element.26), channel_id=1, source_target_pairs={{0,8},{8,0},{16,24},{24,16},{1,9},{9,1},{17,25},{25,17},{2,10},{10... | collective-permute-start | bytes 3145736 | tf_op jit(solution)/shard_map/ppermute | solution.py:13
  29.1 51.4 %copy-start.8 = (bf16[1,64,8192]{2,1,0:T(8,128)(2,1)S(1)}, bf16[1,64,8192]{2,1,0:T(8,128)(2,1)}, u32[]{:S(2)}) copy-start(bf16[1,64,8192]{2,1,0:T(8,128)(2,1)} %param.9) | copy-start | bytes 3145732
  52.1 21.6 %copy-start.6 = (bf16[64,8192]{1,0:T(8,128)(2,1)}, bf16[64,8192]{1,0:T(8,128)(2,1)S(1)}, u32[]{:S(2)}) copy-start(bf16[64,8192]{1,0:T(8,128)(2,1)S(1)} %collective-permute-done.2) | copy-start | bytes 3145732
  73.7 1.0 copy-start.7
  80.6 1.3 copy-start.2
  81.9 1.0 copy-start.4
  83.9 58.3 %all-to-all-start = ((bf16[64,8,1024]{2,0,1:T(8,128)(2,1)}), bf16[64,8,1024]{2,0,1:T(8,128)(2,1)}, u32[]{:S(2)}, u32[]{:S(2)}) async-start(bf16[64,8,1024]{2,0,1:T(8,128)(2,1)} %bitcast.45), calls=%async_computation | async-start | bytes 2097152 | tf_op jit(solution)/shard_map/all_to_all | solution.py:49
  88.9 28.2 %collective-permute-start.5 = (bf16[64,8192]{1,0:T(8,128)(2,1)}, bf16[64,8192]{1,0:T(8,128)(2,1)}, u32[]{:S(2)}, u32[]{:S(2)}) collective-permute-start(bf16[64,8192]{1,0:T(8,128)(2,1)} %get-tuple-element.20), channel_id=1, source_target_pairs={{8,0},{16,8},{24,16},{9,1},{17,9},{25,17},{10,2},{18,10},{26,18},{... | collective-permute-start | bytes 3145736 | tf_op jit(solution)/shard_map/ppermute | solution.py:23
  90.2 49.3 %collective-permute-start.4 = (bf16[64,8192]{1,0:T(8,128)(2,1)}, bf16[64,8192]{1,0:T(8,128)(2,1)}, u32[]{:S(2)}, u32[]{:S(2)}) collective-permute-start(bf16[64,8192]{1,0:T(8,128)(2,1)} %get-tuple-element.24), channel_id=1, source_target_pairs={{8,0},{16,8},{24,16},{9,1},{17,9},{25,17},{10,2},{18,10},{26,18},{... | collective-permute-start | bytes 3145736 | tf_op jit(solution)/shard_map/ppermute | solution.py:23
  91.7 93.7 %collective-permute-start.3 = (bf16[64,8192]{1,0:T(8,128)(2,1)}, bf16[64,8192]{1,0:T(8,128)(2,1)}, u32[]{:S(2)}, u32[]{:S(2)}) collective-permute-start(bf16[64,8192]{1,0:T(8,128)(2,1)} %copy-done.4), channel_id=1, source_target_pairs={{8,0},{16,8},{24,16},{9,1},{17,9},{25,17},{10,2},{18,10},{26,18},{... | collective-permute-start | bytes 3145736 | tf_op jit(solution)/shard_map/ppermute | solution.py:23
  142.2 43.2 %copy-start.5 = (bf16[64,8192]{1,0:T(8,128)(2,1)S(1)}, bf16[64,8192]{1,0:T(8,128)(2,1)}, u32[]{:S(2)}) copy-start(bf16[64,8192]{1,0:T(8,128)(2,1)} %copy-done.4) | copy-start | bytes 3145732
  142.2 43.2 %collective-permute-start.6 = (bf16[8,64,1024]{2,1,0:T(8,128)(2,1)}, bf16[8,64,1024]{2,1,0:T(8,128)(2,1)}, u32[]{:S(2)}, u32[]{:S(2)}) collective-permute-start(bf16[8,64,1024]{2,1,0:T(8,128)(2,1)} %bitcast.11), channel_id=1, source_target_pairs={{0,8},{8,16},{16,24},{24,0},{1,9},{9,17},{17,25},{25,1},{2,10},{10... | collective-permute-start | bytes 3145736 | tf_op jit(solution)/shard_map/ppermute | solution.py:59
  150.7 56.4 %collective-permute-start.7 = (bf16[8,64,1024]{2,1,0:T(8,128)(2,1)}, bf16[8,64,1024]{2,1,0:T(8,128)(2,1)}, u32[]{:S(2)}, u32[]{:S(2)}) collective-permute-start(bf16[8,64,1024]{2,1,0:T(8,128)(2,1)} %bitcast.11), channel_id=1, source_target_pairs={{0,24},{8,0},{16,8},{24,16},{1,25},{9,1},{17,9},{25,17},{2,26},{10... | collective-permute-start | bytes 3145736 | tf_op jit(solution)/shard_map/ppermute | solution.py:62
  185.4 44.6 %collective-permute-start.8 = (bf16[8,64,1024]{2,1,0:T(8,128)(2,1)}, bf16[8,64,1024]{2,1,0:T(8,128)(2,1)}, u32[]{:S(2)}, u32[]{:S(2)}) collective-permute-start(bf16[8,64,1024]{2,1,0:T(8,128)(2,1)} %collective-permute-done.6), channel_id=1, source_target_pairs={{0,8},{8,16},{16,24},{24,0},{1,9},{9,17},{17,25},{25,1},{2,10},{10... | collective-permute-start | bytes 3145736 | tf_op jit(solution)/shard_map/ppermute | solution.py:59
  188.5 6.7 %copy-start.3 = (f32[86,8192]{1,0:T(8,128)S(1)}, f32[86,8192]{1,0:T(8,128)}, u32[]{:S(2)}) copy-start(f32[86,8192]{1,0:T(8,128)} %get-tuple-element.29) | copy-start | bytes 8454148
  232.3 10.6 %copy-start.1 = (bf16[1024,256]{1,0:T(8,128)(2,1)S(1)}, bf16[1024,256]{1,0:T(8,128)(2,1)}, u32[]{:S(2)}) copy-start(bf16[1024,256]{1,0:T(8,128)(2,1)} %param.7) | copy-start | bytes 1572868
Sparse Core Ops, SparseCore 0:
  28.5 49.5 all-gather.1
